TPU v7x, 128 devices: a whole 4x4x4 slice. The times are simulated.
128 devices in a mesh: row: 16 (over z, y), col: 8 (over x, core).
Axes of the slice: x: 4, y: 4, z: 4, core: 2. Of those that a mesh axis runs over, the one named last changes fastest.
Arguments:
- source_cells: float32 [32768, 64], P(('row', 'col')), may hold values from -6 to 6
- target_cells: float32 [16384, 64], P(('col', 'row')), may hold values from -6 to 6
- source_mass: float32 [32768], P(('row', 'col')), may hold values from 0.001 to 1000
- target_mass: float32 [16384], P(('col', 'row')), may hold values from 0.001 to 1000
- support: int32 [32, 16], P('row', 'col'), may hold values from 0 to 1, as said below
Outputs:
- source_potential: float32 [32768], P('row')
- target_potential: float32 [16384], P('col')
Inputs may be any that keep to these rules, and one draw needn't show every extreme that they name: Every source block has at least one supported target block, and every target block has at least one supported source block; the support is uneven from block to block.
All inputs are finite; a program needn't handle non-finite values.
Results may differ from a plain program's by a relative error of at most 0.0003.
Values sent between devices are 32-bit elements; how exact they have to be, the bound alone decides.
A program may use at most 128 MiB of HBM per device.

v0:
```python
import math

import jax
import jax.numpy as jnp
from jax import lax
from jax.experimental import pallas as pl
from jax.experimental.pallas import tpu as pltpu
from jax.sharding import PartitionSpec as P

MESH = pl.DeviceIdType.MESH
LATENT = 64
ROWS = 16
COLS = 8
LANES = 128
GROUPS = 16
TERMS = 384
EPSILON = 0.02
NEGATIVE = -1e30
SCALE = math.sqrt(2.0 * math.log2(math.e) / (LATENT * EPSILON))
BACK = EPSILON * math.log(2.0)
FAR_FIRST = tuple(sorted(range(1, ROWS), key=lambda k: -((0, 1, 2, 1)[k & 3] + (0, 1, 2, 1)[k >> 2])))


def pieces(value):
    high = value.astype(jnp.bfloat16)
    rest = value - high.astype(jnp.float32)
    mid = rest.astype(jnp.bfloat16)
    low = (rest - mid.astype(jnp.float32)).astype(jnp.bfloat16)
    return high, mid, low


def tree(op, parts):
    parts = list(parts)
    while len(parts) > 1:
        parts = [
            op(parts[k], parts[k + 1]) if k + 1 < len(parts) else parts[k]
            for k in range(0, len(parts), 2)
        ]
    return parts[0]


def gray(i):
    return i ^ (i // 2)


def kernel(
    x_hbm, y_hbm, a_hbm, b_hbm, support_hbm, u_ref, v_ref,
    x_ref, y_ref, a_ref, b_ref, support_ref,
    xbuf, ybuf, left, right, score, upart, vpart, ucol, vbias,
    row_peak, row_total, col_peak, col_total,
    in_sem, x_send, x_recv, relay_send, relay_recv, y_send, y_recv, u_send, u_recv, v_send, v_recv,
):
    row = lax.axis_index("row")
    col = lax.axis_index("col")
    my_z = row // 4
    my_x = col // 2

    loads = [
        pltpu.make_async_copy(src, dst, in_sem.at[k])
        for k, (src, dst) in enumerate(
            ((x_hbm, x_ref), (y_hbm, y_ref), (a_hbm, a_ref), (b_hbm, b_ref), (support_hbm, support_ref))
        )
    ]
    for load in loads:
        load.start()

    barrier = pltpu.get_barrier_semaphore()
    for k in FAR_FIRST:
        pl.semaphore_signal(barrier, inc=1, device_id=(row ^ k, col), device_id_type=MESH)
    for k in range(1, COLS):
        pl.semaphore_signal(barrier, inc=1, device_id=(row, col ^ k), device_id_type=MESH)

    def bias(a, b):
        return jnp.where(support_ref[a, b] == 1, jnp.float32(0.0), jnp.float32(NEGATIVE))

    def over_row(ref, send, recv, k):
        return pltpu.make_async_remote_copy(
            src_ref=ref.at[row], dst_ref=ref.at[row], send_sem=send.at[k], recv_sem=recv.at[k],
            device_id=(row ^ k, col), device_id_type=MESH,
        )

    def over_col(ref, send, recv, k):
        return pltpu.make_async_remote_copy(
            src_ref=ref.at[col], dst_ref=ref.at[col], send_sem=send.at[k], recv_sem=recv.at[k],
            device_id=(row, col ^ k), device_id_type=MESH,
        )

    def relay(owner, k):
        return pltpu.make_async_remote_copy(
            src_ref=xbuf.at[owner], dst_ref=xbuf.at[owner], send_sem=relay_send.at[k], recv_sem=relay_recv.at[k],
            device_id=(row, col ^ 1), device_id_type=MESH,
        )

    for load in loads:
        load.wait()
    x_cells = x_ref[...] * SCALE
    x_half = 0.5 * jnp.sum(x_cells * x_cells, axis=0, keepdims=True)
    both = jnp.concatenate([x_cells[:, 0:LANES], x_cells[:, LANES : 2 * LANES]], axis=0)
    xbuf[col, 0:LANES, :] = both.T
    xbuf[col, LANES : LANES + 8, :] = jnp.concatenate(
        [jnp.log2(a_ref[...]), x_half[:, 0:LANES], x_half[:, LANES : 2 * LANES], jnp.zeros((4, LANES), jnp.float32)],
        axis=0,
    )
    y_cells = y_ref[...] * SCALE
    ybuf[row, 0:LATENT, :] = y_cells
    ybuf[row, LATENT : LATENT + 8, :] = jnp.concatenate(
        [
            jnp.log2(b_ref[...]),
            0.5 * jnp.sum(y_cells * y_cells, axis=0, keepdims=True),
            jnp.zeros((6, LANES), jnp.float32),
        ],
        axis=0,
    )

    def clear(i, carry):
        at = pl.ds(pl.multiple_of(i * LANES, LANES), LANES)
        row_peak[at, :] = jnp.full((LANES, LANES), 3.0 * NEGATIVE, jnp.float32)
        row_total[at, :] = jnp.zeros((LANES, LANES), jnp.float32)
        return carry

    lax.fori_loop(0, GROUPS, clear, 0)

    pl.semaphore_wait(barrier, COLS + ROWS - 2)

    for k in (4, 2, 6, 1):
        over_col(xbuf, x_send, x_recv, k).start()
    for k in FAR_FIRST:
        over_row(ybuf, y_send, y_recv, k).start()

    lower = lax.broadcasted_iota(jnp.int32, (LANES, LANES), 1) < LATENT
    eye = lax.broadcasted_iota(jnp.int32, (LANES, LANES), 0) == lax.broadcasted_iota(jnp.int32, (LANES, LANES), 1)

    def build_right(level):
        zg = my_z ^ gray(level)
        for yy in range(4):
            k = 4 * gray(level) + yy
            if k > 0:
                over_row(ybuf, y_send, y_recv, k).wait_recv()
        for yy in range(4):
            high, mid, low = pieces(ybuf[zg * 4 + yy, 0:LATENT, :])
            at = slice(yy * LANES, (yy + 1) * LANES)
            for place, piece in enumerate((high, mid, high, mid, low, high)):
                right[zg, LATENT * place : LATENT * (place + 1), at] = piece
            start = -ybuf[zg * 4 + yy, LATENT + 1 : LATENT + 2, :]
            for a in range(2):
                vbias[a, zg * 4 + yy] = jnp.broadcast_to(start + bias(a, zg // 2), (8, LANES))

    def build_left(level):
        xg = my_x ^ gray(level)
        for e in range(2):
            packed = xbuf[2 * xg + e, 0:LANES, :]
            turned = pltpu.roll(packed, LATENT, 1)
            for half in range(2):
                if half == 0:
                    twice = jnp.where(lower, packed, turned)
                else:
                    twice = jnp.where(lower, turned, packed)
                high, mid, low = pieces(twice)
                at = slice((2 * e + half) * LANES, (2 * e + half + 1) * LANES)
                left[xg, at, 0:LANES] = high
                left[xg, at, LANES : 2 * LANES] = mid
                left[xg, at, 2 * LANES : 3 * LANES] = jnp.where(
                    lower, high.astype(jnp.float32), low.astype(jnp.float32)
                ).astype(jnp.bfloat16)

    def tile(xg, zg):
        pot = [vbias[xg // 2, zg * 4 + c] for c in range(4)]
        base = xg * 512
        for i in range(4):
            res = jnp.dot(
                left[xg, i * LANES : (i + 1) * LANES, :], right[zg], preferred_element_type=jnp.float32
            )
            for c in range(4):
                at = pl.ds(pl.multiple_of(base + i * LANES, LANES), LANES)
                score[zg * 4 + c, at, :] = res[:, c * LANES : (c + 1) * LANES]
            for q in range(GROUPS):
                at = pl.ds(pl.multiple_of(base + i * LANES + 8 * q, 8), 8)
                t = [res[8 * q : 8 * q + 8, c * LANES : (c + 1) * LANES] + pot[c] for c in range(4)]
                old = row_peak[at, :]
                new = jnp.maximum(tree(jnp.maximum, t), old)
                total = tree(jnp.add, [jnp.exp2(value - new) for value in t])
                row_total[at, :] = row_total[at, :] * jnp.exp2(old - new) + total
                row_peak[at, :] = new

    def finish_rows(step, xg, block, peak, total):
        peak, total = peak.T, total.T
        top = jnp.max(peak, axis=0, keepdims=True)
        whole = jnp.sum(total * jnp.exp2(peak - top), axis=0, keepdims=True)
        upart[step, xg, col, pl.ds(block, 1), :] = top + jnp.log2(whole)

    def send_u(step, xg):
        for k in range(1, COLS):
            over_col(upart.at[step, xg], u_send.at[step, xg], u_recv.at[step, xg], k).start()

    for k in (2, 6):
        over_col(xbuf, x_send, x_recv, k).wait_recv()
        relay(col ^ k, k).start()
    over_col(xbuf, x_send, x_recv, 1).wait_recv()
    build_left(0)
    build_right(0)
    tile(my_x, my_z)
    over_col(xbuf, x_send, x_recv, 4).wait_recv()
    relay(col ^ 4, 4).start()
    build_right(1)
    relay(col ^ 3, 2).wait_recv()
    build_left(1)

    def several(count, xs, zs):
        def body(i, carry):
            tile(xs(i), zs(i))
            return carry

        lax.fori_loop(0, count, body, 0)

    several(3, lambda i: my_x ^ gray((i + 1) // 2), lambda i: my_z ^ gray(1 - i % 2))
    build_right(2)
    relay(col ^ 7, 6).wait_recv()
    build_left(2)
    several(5, lambda i: my_x ^ gray(jnp.minimum(i, 2)), lambda i: my_z ^ gray(jnp.where(i < 2, 2, i - 2)))
    relay(col ^ 5, 4).wait_recv()
    build_left(3)
    several(3, lambda i: my_x ^ gray(3), lambda i: my_z ^ gray(i))
    build_right(3)

    def last(xg, carry):
        tile(xg, my_z ^ gray(3))
        for block in range(4):
            at = pl.ds(pl.multiple_of(xg * 512 + block * LANES, LANES), LANES)
            finish_rows(0, xg, block, row_peak[at, :], row_total[at, :])
        send_u(0, xg)
        return carry

    lax.fori_loop(0, 4, last, 0)

    def combine_u(step, xg):
        for k in range(1, COLS):
            over_col(upart.at[step, xg], u_send.at[step, xg], u_recv.at[step, xg], k).wait_recv()
        parts = [upart[step, xg, k] for k in range(COLS)]
        top = tree(jnp.maximum, parts)
        total = tree(jnp.add, [jnp.exp2(p - top) for p in parts])
        mass = jnp.concatenate([xbuf[2 * xg + e, LANES : LANES + 2, :] for e in range(2)], axis=0)
        pot = mass - (top + jnp.log2(total))
        for block in range(4):
            spread = jnp.where(eye, jnp.broadcast_to(pot[block : block + 1, :], (LANES, LANES)), 0.0)
            wide = jnp.sum(spread, axis=1, keepdims=True)
            ucol[block * LANES : (block + 1) * LANES, :] = jnp.broadcast_to(wide, (LANES, LANES))
        if step == 1:
            half = jnp.concatenate([xbuf[2 * xg + e, LANES + 2 : LANES + 4, :] for e in range(2)], axis=0)
            u_ref[pl.ds(xg * 4, 4), :] = BACK * (pot + half)

    def column_pass(step):
        col_peak[...] = jnp.full((GROUPS, 8, LANES), 3.0 * NEGATIVE, jnp.float32)
        col_total[...] = jnp.zeros((GROUPS, 8, LANES), jnp.float32)

        def body(t, carry):
            xg, quad = t // 4, t % 4

            @pl.when(quad == 0)
            def _():
                combine_u(step, xg)

            live = bias(xg // 2, quad // 2)
            base = xg * 512
            peaks = [[col_peak[4 * quad + c]] for c in range(4)]
            totals = [[col_total[4 * quad + c]] for c in range(4)]
            for g in range(4):
                pots = [ucol[g * LANES + 8 * k : g * LANES + 8 * k + 8, :] for k in range(GROUPS)]
                for c in range(4):
                    values = [
                        score[4 * quad + c, pl.ds(pl.multiple_of(base + g * LANES + 8 * k, 8), 8), :] + pots[k]
                        for k in range(GROUPS)
                    ]
                    peak = tree(jnp.maximum, values)
                    totals[c].append(tree(jnp.add, [jnp.exp2(value - peak) for value in values]))
                    peaks[c].append(peak + live)
            for c in range(4):
                top = tree(jnp.maximum, peaks[c])
                total = tree(jnp.add, [q * jnp.exp2(p - top) for p, q in zip(peaks[c], totals[c])])
                col_peak[4 * quad + c] = top
                col_total[4 * quad + c] = total

            @pl.when(xg == 3)
            def _():
                lines = []
                for c in range(4):
                    peak, total = col_peak[4 * quad + c], col_total[4 * quad + c]
                    top = jnp.max(peak, axis=0, keepdims=True)
                    whole = jnp.sum(total * jnp.exp2(peak - top), axis=0, keepdims=True)
                    lines.append(top + jnp.log2(whole))
                vpart[step, quad // 2, row, pl.ds(quad % 2 * 4, 4), :] = jnp.concatenate(lines, axis=0)

            @pl.when(jnp.logical_and(xg == 3, quad % 2 == 1))
            def _():
                half = quad // 2
                for k in FAR_FIRST:
                    over_row(vpart.at[step, half], v_send.at[step, half], v_recv.at[step, half], k).start()

            return carry

        lax.fori_loop(0, GROUPS, body, 0)

    def combine_v(step, half):
        for k in FAR_FIRST[::-1]:
            over_row(vpart.at[step, half], v_send.at[step, half], v_recv.at[step, half], k).wait_recv()
        parts = [vpart[step, half, k] for k in range(ROWS)]
        top = tree(jnp.maximum, parts)
        total = tree(jnp.add, [jnp.exp2(p - top) for p in parts])
        mass = jnp.concatenate([ybuf[8 * half + k, LATENT : LATENT + 1, :] for k in range(8)], axis=0)
        return mass - (top + jnp.log2(total))

    column_pass(0)
    for half in range(2):
        pot = combine_v(0, half)
        for a in range(2):
            shifted = pot + bias(a, half)
            for c in range(8):
                vbias[a, 8 * half + c] = jnp.broadcast_to(shifted[c : c + 1, :], (8, LANES))

    def row_block(t, carry):
        xg, block = t // 4, t % 4
        pot = [vbias[xg // 2, c] for c in range(GROUPS)]
        peaks, totals = [], []
        for k in range(GROUPS):
            at = pl.ds(pl.multiple_of(t * LANES + 8 * k, 8), 8)
            values = [score[c, at, :] + pot[c] for c in range(GROUPS)]
            peak = tree(jnp.maximum, values)
            totals.append(tree(jnp.add, [jnp.exp2(value - peak) for value in values]))
            peaks.append(peak)
        finish_rows(1, xg, block, jnp.concatenate(peaks, axis=0), jnp.concatenate(totals, axis=0))

        @pl.when(block == 3)
        def _():
            send_u(1, xg)

        return carry

    lax.fori_loop(0, GROUPS, row_block, 0)
    column_pass(1)
    for half in range(2):
        pot = combine_v(1, half)
        y_half = jnp.concatenate([ybuf[8 * half + k, LATENT + 1 : LATENT + 2, :] for k in range(8)], axis=0)
        v_ref[8 * half : 8 * half + 8, :] = BACK * (pot + y_half)

    for k in FAR_FIRST:
        over_row(ybuf, y_send, y_recv, k).wait_send()
        for step in range(2):
            for half in range(2):
                over_row(vpart.at[step, half], v_send.at[step, half], v_recv.at[step, half], k).wait_send()
    for k in (4, 2, 6, 1):
        over_col(xbuf, x_send, x_recv, k).wait_send()
    for k in (2, 6, 4):
        relay(col ^ k, k).wait_send()
    for k in range(1, COLS):
        for step in range(2):
            for xg in range(4):
                over_col(upart.at[step, xg], u_send.at[step, xg], u_recv.at[step, xg], k).wait_send()


def local(source_cells, target_cells, source_mass, target_mass, support):
    vmem = pl.BlockSpec(memory_space=pltpu.VMEM)
    hbm = pl.BlockSpec(memory_space=pl.ANY)
    u, v = pl.pallas_call(
        kernel,
        out_shape=(
            jax.ShapeDtypeStruct((GROUPS, LANES), jnp.float32),
            jax.ShapeDtypeStruct((GROUPS, LANES), jnp.float32),
        ),
        in_specs=[hbm] * 5,
        out_specs=(vmem, vmem),
        scratch_shapes=[
            pltpu.VMEM((LATENT, 256), jnp.float32),
            pltpu.VMEM((LATENT, LANES), jnp.float32),
            pltpu.VMEM((2, LANES), jnp.float32),
            pltpu.VMEM((1, LANES), jnp.float32),
            pltpu.SMEM((2, 2), jnp.int32),
            pltpu.VMEM((COLS, LANES + 8, LANES), jnp.float32),
            pltpu.VMEM((ROWS, LATENT + 8, LANES), jnp.float32),
            pltpu.VMEM((4, 512, TERMS), jnp.bfloat16),
            pltpu.VMEM((4, TERMS, 512), jnp.bfloat16),
            pltpu.VMEM((GROUPS, 2048, LANES), jnp.float32),
            pltpu.VMEM((2, 4, COLS, 4, LANES), jnp.float32),
            pltpu.VMEM((2, 2, ROWS, 8, LANES), jnp.float32),
            pltpu.VMEM((512, LANES), jnp.float32),
            pltpu.VMEM((2, GROUPS, 8, LANES), jnp.float32),
            pltpu.VMEM((2048, LANES), jnp.float32),
            pltpu.VMEM((2048, LANES), jnp.float32),
            pltpu.VMEM((GROUPS, 8, LANES), jnp.float32),
            pltpu.VMEM((GROUPS, 8, LANES), jnp.float32),
            pltpu.SemaphoreType.DMA((5,)),
            pltpu.SemaphoreType.DMA((COLS,)),
            pltpu.SemaphoreType.DMA((COLS,)),
            pltpu.SemaphoreType.DMA((COLS,)),
            pltpu.SemaphoreType.DMA((COLS,)),
            pltpu.SemaphoreType.DMA((ROWS,)),
            pltpu.SemaphoreType.DMA((ROWS,)),
            pltpu.SemaphoreType.DMA((2, 4, COLS)),
            pltpu.SemaphoreType.DMA((2, 4, COLS)),
            pltpu.SemaphoreType.DMA((2, 2, ROWS)),
            pltpu.SemaphoreType.DMA((2, 2, ROWS)),
        ],
        compiler_params=pltpu.CompilerParams(
            collective_id=0, has_side_effects=True, vmem_limit_bytes=48 * 1024 * 1024
        ),
        name="sinkhorn",
    )(
        source_cells.T,
        target_cells.T,
        source_mass.reshape(2, LANES),
        target_mass.reshape(1, LANES),
        support,
    )
    return u.reshape(2048), v.reshape(2048)


def solution(mesh):
    return jax.shard_map(
        local,
        mesh=mesh,
        in_specs=(
            P(("row", "col"), None),
            P(("col", "row"), None),
            P(("row", "col")),
            P(("col", "row")),
            P("row", "col"),
        ),
        out_specs=(P("row"), P("col")),
        check_vma=False,
    )
```

profile of v0, /device:TPU:1, one launch (start us, length us, event | category | flops | bytes accessed | tf_op | source)
XLA Modules:
  0.0 58.6 jit_solution(13065771256178168105)
XLA Ops:
  0.6 0.0 copy-start.3
  0.6 0.0 copy-start.2
  0.7 0.0 copy-start.4
  0.7 0.7 %copy-done.3 = s32[2,2]{1,0:T(2,128)S(1)} copy-done((s32[2,2]{1,0:T(2,128)S(1)}, s32[2,2]{1,0:T(2,128)}, u32[]{:S(2)}) %copy-start.3) | copy-done | bytes 40
  1.3 0.0 copy-done.2
  1.3 0.0 copy-done.4
  1.3 0.0 copy-start
  1.3 0.8 %copy-done = f32[256,64]{0,1:T(8,128)S(1)} copy-done((f32[256,64]{0,1:T(8,128)S(1)}, f32[256,64]{0,1:T(8,128)}, u32[]{:S(2)}) %copy-start) | copy-done | bytes 65560
  2.2 0.0 copy-start.1
  2.2 0.8 %copy-done.1 = f32[128,64]{0,1:T(8,128)S(1)} copy-done((f32[128,64]{0,1:T(8,128)S(1)}, f32[128,64]{0,1:T(8,128)}, u32[]{:S(2)}) %copy-start.1) | copy-done | bytes 32792
  2.9 54.4 %sinkhorn.1 = (f32[16,128]{1,0:T(8,128)S(1)}, f32[16,128]{1,0:T(8,128)S(1)}) custom-call(f32[64,256]{1,0:T(8,128)S(1)} %bitcast.6, f32[64,128]{1,0:T(8,128)S(1)} %bitcast.7, f32[2,128]{1,0:T(2,128)S(1)} %bitcast.10, f32[1,128]{1,0:T(1,128)S(1)} %bitcast.11, s32[2,2]{1,0:T(2,128)S(1)} %copy-done.3), custom_call_target="tpu_custom_call" | custom-call | tf_op jit(solution)/shard_map/sinkhorn/pallas_call | solution.py:362
  57.4 0.6 %copy.9 = f32[2048]{0:T(1024)} copy(f32[2048]{0:T(1024)S(1)} %bitcast.9) | data formatting | bytes 16384
  58.0 0.6 %copy.10 = f32[2048]{0:T(1024)} copy(f32[2048]{0:T(1024)S(1)} %bitcast.8) | data formatting | bytes 16384
Async XLA Ops:
  0.6 0.7 %copy-start.3 = (s32[2,2]{1,0:T(2,128)S(1)}, s32[2,2]{1,0:T(2,128)}, u32[]{:S(2)}) copy-start(s32[2,2]{1,0:T(2,128)} %support_hbm.1) | copy-start | bytes 52
  0.6 0.7 %copy-start.2 = (f32[256]{0:T(256)S(1)}, f32[256]{0:T(256)}, u32[]{:S(2)}) copy-start(f32[256]{0:T(256)} %param.7) | copy-start | bytes 3076
  0.7 0.7 %copy-start.4 = (f32[128]{0:T(128)S(1)}, f32[128]{0:T(128)}, u32[]{:S(2)}) copy-start(f32[128]{0:T(128)} %param.8) | copy-start | bytes 1540
  1.3 0.8 %copy-start = (f32[256,64]{0,1:T(8,128)S(1)}, f32[256,64]{0,1:T(8,128)}, u32[]{:S(2)}) copy-start(f32[256,64]{0,1:T(8,128)} %param.5) | copy-start | bytes 196612
  2.2 0.8 %copy-start.1 = (f32[128,64]{0,1:T(8,128)S(1)}, f32[128,64]{0,1:T(8,128)}, u32[]{:S(2)}) copy-start(f32[128,64]{0,1:T(8,128)} %param.6) | copy-start | bytes 98308
where the time goes:
time: 59 us; the launch traced here: 58.6 us
  Pallas kernels  54.4 us (92%)
  local copies, waits for them, and re-layouts  3.47 us (6%)
  between operations  0.67 us (1%)
    pallas_call x1, Pallas kernels, local(): pl.pallas_call(kernel, out_shape=(jax.ShapeDtypeStruct((GROUPS, LANES), j...  54.4 us
    unnamed x12, local copies, waits for them, and re-layouts  3.47 us

commit v1 on v0

--- a/solution.py
+++ b/solution.py
@@ -48,7 +48,7 @@
     x_ref, y_ref, a_ref, b_ref, support_ref,
     xbuf, ybuf, left, right, score, upart, vpart, ucol, vbias,
     row_peak, row_total, col_peak, col_total,
-    in_sem, x_send, x_recv, relay_send, relay_recv, y_send, y_recv, u_send, u_recv, v_send, v_recv,
+    in_sem, sent, x_recv, relay_recv, y_recv, u_recv, v_recv,
 ):
     row = lax.axis_index("row")
     col = lax.axis_index("col")
@@ -75,21 +75,24 @@
 
     def over_row(ref, send, recv, k):
         return pltpu.make_async_remote_copy(
-            src_ref=ref.at[row], dst_ref=ref.at[row], send_sem=send.at[k], recv_sem=recv.at[k],
+            src_ref=ref.at[row], dst_ref=ref.at[row], send_sem=send, recv_sem=recv,
             device_id=(row ^ k, col), device_id_type=MESH,
         )
 
     def over_col(ref, send, recv, k):
         return pltpu.make_async_remote_copy(
-            src_ref=ref.at[col], dst_ref=ref.at[col], send_sem=send.at[k], recv_sem=recv.at[k],
+            src_ref=ref.at[col], dst_ref=ref.at[col], send_sem=send, recv_sem=recv,
             device_id=(row, col ^ k), device_id_type=MESH,
         )
 
     def relay(owner, k):
         return pltpu.make_async_remote_copy(
-            src_ref=xbuf.at[owner], dst_ref=xbuf.at[owner], send_sem=relay_send.at[k], recv_sem=relay_recv.at[k],
+            src_ref=xbuf.at[owner], dst_ref=xbuf.at[owner], send_sem=sent.at[1], recv_sem=relay_recv.at[k // 2],
             device_id=(row, col ^ 1), device_id_type=MESH,
         )
+
+    def all_of(ref, sem):
+        return pltpu.make_async_copy(ref, ref, sem)
 
     for load in loads:
         load.wait()
@@ -123,19 +126,17 @@
     pl.semaphore_wait(barrier, COLS + ROWS - 2)
 
     for k in (4, 2, 6, 1):
-        over_col(xbuf, x_send, x_recv, k).start()
+        over_col(xbuf, sent.at[0], x_recv.at[k // 2], k).start()
     for k in FAR_FIRST:
-        over_row(ybuf, y_send, y_recv, k).start()
+        over_row(ybuf, sent.at[2], y_recv.at[k // 4], k).start()
 
     lower = lax.broadcasted_iota(jnp.int32, (LANES, LANES), 1) < LATENT
     eye = lax.broadcasted_iota(jnp.int32, (LANES, LANES), 0) == lax.broadcasted_iota(jnp.int32, (LANES, LANES), 1)
 
     def build_right(level):
         zg = my_z ^ gray(level)
-        for yy in range(4):
-            k = 4 * gray(level) + yy
-            if k > 0:
-                over_row(ybuf, y_send, y_recv, k).wait_recv()
+        count = 3 if level == 0 else 4
+        all_of(ybuf.at[0:count], y_recv.at[gray(level)]).wait()
         for yy in range(4):
             high, mid, low = pieces(ybuf[zg * 4 + yy, 0:LATENT, :])
             at = slice(yy * LANES, (yy + 1) * LANES)
@@ -190,16 +191,16 @@
 
     def send_u(step, xg):
         for k in range(1, COLS):
-            over_col(upart.at[step, xg], u_send.at[step, xg], u_recv.at[step, xg], k).start()
+            over_col(upart.at[step, xg], sent.at[3 + step], u_recv.at[step, xg], k).start()
 
     for k in (2, 6):
-        over_col(xbuf, x_send, x_recv, k).wait_recv()
+        over_col(xbuf, sent.at[0], x_recv.at[k // 2], k).wait_recv()
         relay(col ^ k, k).start()
-    over_col(xbuf, x_send, x_recv, 1).wait_recv()
+    over_col(xbuf, sent.at[0], x_recv.at[0], 1).wait_recv()
     build_left(0)
     build_right(0)
     tile(my_x, my_z)
-    over_col(xbuf, x_send, x_recv, 4).wait_recv()
+    over_col(xbuf, sent.at[0], x_recv.at[2], 4).wait_recv()
     relay(col ^ 4, 4).start()
     build_right(1)
     relay(col ^ 3, 2).wait_recv()
@@ -233,8 +234,7 @@
     lax.fori_loop(0, 4, last, 0)
 
     def combine_u(step, xg):
-        for k in range(1, COLS):
-            over_col(upart.at[step, xg], u_send.at[step, xg], u_recv.at[step, xg], k).wait_recv()
+        all_of(upart.at[step, xg, 0 : COLS - 1], u_recv.at[step, xg]).wait()
         parts = [upart[step, xg, k] for k in range(COLS)]
         top = tree(jnp.maximum, parts)
         total = tree(jnp.add, [jnp.exp2(p - top) for p in parts])
@@ -246,7 +246,7 @@
             ucol[block * LANES : (block + 1) * LANES, :] = jnp.broadcast_to(wide, (LANES, LANES))
         if step == 1:
             half = jnp.concatenate([xbuf[2 * xg + e, LANES + 2 : LANES + 4, :] for e in range(2)], axis=0)
-            u_ref[pl.ds(xg * 4, 4), :] = BACK * (pot + half)
+            u_ref[pl.ds(xg * 4, 4), :] = (pot + half)
 
     def column_pass(step):
         col_peak[...] = jnp.full((GROUPS, 8, LANES), 3.0 * NEGATIVE, jnp.float32)
@@ -293,15 +293,14 @@
             def _():
                 half = quad // 2
                 for k in FAR_FIRST:
-                    over_row(vpart.at[step, half], v_send.at[step, half], v_recv.at[step, half], k).start()
+                    over_row(vpart.at[step, half], sent.at[5 + step], v_recv.at[step, half], k).start()
 
             return carry
 
         lax.fori_loop(0, GROUPS, body, 0)
 
     def combine_v(step, half):
-        for k in FAR_FIRST[::-1]:
-            over_row(vpart.at[step, half], v_send.at[step, half], v_recv.at[step, half], k).wait_recv()
+        all_of(vpart.at[step, half, 0 : ROWS - 1], v_recv.at[step, half]).wait()
         parts = [vpart[step, half, k] for k in range(ROWS)]
         top = tree(jnp.maximum, parts)
         total = tree(jnp.add, [jnp.exp2(p - top) for p in parts])
@@ -336,29 +335,21 @@
 
     lax.fori_loop(0, GROUPS, row_block, 0)
     column_pass(1)
+    all_of(xbuf.at[0:4], sent.at[0]).wait()
+    all_of(xbuf.at[0:3], sent.at[1]).wait()
+    all_of(ybuf.at[0 : ROWS - 1], sent.at[2]).wait()
+    for step in range(2):
+        all_of(upart.at[step, :, 0 : COLS - 1], sent.at[3 + step]).wait()
+        all_of(vpart.at[step, :, 0 : ROWS - 1], sent.at[5 + step]).wait()
     for half in range(2):
         pot = combine_v(1, half)
         y_half = jnp.concatenate([ybuf[8 * half + k, LATENT + 1 : LATENT + 2, :] for k in range(8)], axis=0)
-        v_ref[8 * half : 8 * half + 8, :] = BACK * (pot + y_half)
-
-    for k in FAR_FIRST:
-        over_row(ybuf, y_send, y_recv, k).wait_send()
-        for step in range(2):
-            for half in range(2):
-                over_row(vpart.at[step, half], v_send.at[step, half], v_recv.at[step, half], k).wait_send()
-    for k in (4, 2, 6, 1):
-        over_col(xbuf, x_send, x_recv, k).wait_send()
-    for k in (2, 6, 4):
-        relay(col ^ k, k).wait_send()
-    for k in range(1, COLS):
-        for step in range(2):
-            for xg in range(4):
-                over_col(upart.at[step, xg], u_send.at[step, xg], u_recv.at[step, xg], k).wait_send()
+        v_ref[8 * half : 8 * half + 8, :] = (pot + y_half)
 
 
 def local(source_cells, target_cells, source_mass, target_mass, support):
     vmem = pl.BlockSpec(memory_space=pltpu.VMEM)
-    hbm = pl.BlockSpec(memory_space=pl.ANY)
+    hbm = pl.BlockSpec(memory_space=pltpu.HBM)
     u, v = pl.pallas_call(
         kernel,
         out_shape=(
@@ -387,29 +378,30 @@
             pltpu.VMEM((GROUPS, 8, LANES), jnp.float32),
             pltpu.VMEM((GROUPS, 8, LANES), jnp.float32),
             pltpu.SemaphoreType.DMA((5,)),
-            pltpu.SemaphoreType.DMA((COLS,)),
-            pltpu.SemaphoreType.DMA((COLS,)),
-            pltpu.SemaphoreType.DMA((COLS,)),
-            pltpu.SemaphoreType.DMA((COLS,)),
-            pltpu.SemaphoreType.DMA((ROWS,)),
-            pltpu.SemaphoreType.DMA((ROWS,)),
-            pltpu.SemaphoreType.DMA((2, 4, COLS)),
-            pltpu.SemaphoreType.DMA((2, 4, COLS)),
-            pltpu.SemaphoreType.DMA((2, 2, ROWS)),
-            pltpu.SemaphoreType.DMA((2, 2, ROWS)),
+            pltpu.SemaphoreType.DMA((7,)),
+            pltpu.SemaphoreType.DMA((4,)),
+            pltpu.SemaphoreType.DMA((4,)),
+            pltpu.SemaphoreType.DMA((4,)),
+            pltpu.SemaphoreType.DMA((2, 4)),
+            pltpu.SemaphoreType.DMA((2, 2)),
         ],
         compiler_params=pltpu.CompilerParams(
             collective_id=0, has_side_effects=True, vmem_limit_bytes=48 * 1024 * 1024
         ),
         name="sinkhorn",
     )(
-        source_cells.T,
-        target_cells.T,
-        source_mass.reshape(2, LANES),
-        target_mass.reshape(1, LANES),
-        support,
+        *(
+            pltpu.with_memory_space_constraint(value, pltpu.HBM)
+            for value in (
+                source_cells.T,
+                target_cells.T,
+                source_mass.reshape(2, LANES),
+                target_mass.reshape(1, LANES),
+                support,
+            )
+        )
     )
-    return u.reshape(2048), v.reshape(2048)
+    return BACK * u.reshape(2048), BACK * v.reshape(2048)
 
 
 def solution(mesh):

time: 59 us -> 52.7 us (0.89)
  local copies, waits for them, and re-layouts: 3.47 us -> 0 us
  Pallas kernels: 54.4 us -> 51.2 us
  other arithmetic: 0 us -> 0.61 us
    unnamed x12 -> x0, local copies, waits for them, and re-layouts: 3.47 us -> none
    pallas_call x1, Pallas kernels: 54.4 us -> 51.2 us  [local(): pl.pallas_call(kernel, out_shape=(jax.ShapeDtypeStruct((GROUPS, LANES), j...]
    mul x0 -> x1, other arithmetic: none -> 0.61 us  [local(): return (BACK * u.reshape(2048), BACK * v.reshape(2048))]
where the time goes in v1:
time: 52.7 us; the launch traced here: 52.4 us
  Pallas kernels  51.2 us (97%)
  between operations  0.64 us (1%)
  other arithmetic  0.61 us (1%)
    pallas_call x1, Pallas kernels, local(): pl.pallas_call(kernel, out_shape=(jax.ShapeDtypeStruct((GROUPS, LANES), j...  51.2 us

profile of v1, /device:TPU:1, one launch (start us, length us, event | category | flops | bytes accessed | tf_op | source)
XLA Modules:
  0.0 52.4 jit_solution(13588195685551799457)
XLA Ops:
  0.6 51.2 %sinkhorn.1 = (f32[16,128]{1,0:T(8,128)S(1)}, f32[16,128]{1,0:T(8,128)S(1)}) custom-call(f32[64,256]{1,0:T(8,128)} %bitcast.8, f32[64,128]{1,0:T(8,128)} %bitcast.9, f32[2,128]{1,0:T(2,128)} %bitcast.10, f32[1,128]{1,0:T(1,128)} %bitcast.11, s32[2,2]{1,0:T(2,128)} %support_hbm.1), custom_call_target="tpu_custom_call" | custom-call | tf_op jit(solution)/shard_map/sinkhorn/pallas_call | solution.py:353
  51.8 0.6 %multiply_bitcast_fusion = (f32[2048]{0:T(1024)}, f32[2048]{0:T(1024)}) fusion(f32[16,128]{1,0:T(8,128)S(1)} %get-tuple-element.5, f32[16,128]{1,0:T(8,128)S(1)} %get-tuple-element.4), kind=kLoop, calls=%fused_computation | loop fusion | flops 4096 | bytes 32768 | tf_op jit(solution)/shard_map/mul | solution.py:404

commit v2 on v1

--- a/solution.py
+++ b/solution.py
@@ -127,7 +127,7 @@
 
     for k in (4, 2, 6, 1):
         over_col(xbuf, sent.at[0], x_recv.at[k // 2], k).start()
-    for k in FAR_FIRST:
+    for k in (10, 2, 1, 3, 6, 4, 5, 7, 9, 11, 14, 8, 13, 15, 12):
         over_row(ybuf, sent.at[2], y_recv.at[k // 4], k).start()
 
     lower = lax.broadcasted_iota(jnp.int32, (LANES, LANES), 1) < LATENT
@@ -164,19 +164,22 @@
                     lower, high.astype(jnp.float32), low.astype(jnp.float32)
                 ).astype(jnp.bfloat16)
 
-    def tile(xg, zg):
-        pot = [vbias[xg // 2, zg * 4 + c] for c in range(4)]
+    def tile(xg, zgs):
+        pot = [vbias[xg // 2, zg * 4 + c] for zg in zgs for c in range(4)]
         base = xg * 512
         for i in range(4):
-            res = jnp.dot(
-                left[xg, i * LANES : (i + 1) * LANES, :], right[zg], preferred_element_type=jnp.float32
-            )
-            for c in range(4):
-                at = pl.ds(pl.multiple_of(base + i * LANES, LANES), LANES)
-                score[zg * 4 + c, at, :] = res[:, c * LANES : (c + 1) * LANES]
+            found = []
+            for zg in zgs:
+                res = jnp.dot(
+                    left[xg, i * LANES : (i + 1) * LANES, :], right[zg], preferred_element_type=jnp.float32
+                )
+                for c in range(4):
+                    found.append(res[:, c * LANES : (c + 1) * LANES])
+                    at = pl.ds(pl.multiple_of(base + i * LANES, LANES), LANES)
+                    score[zg * 4 + c, at, :] = found[-1]
             for q in range(GROUPS):
                 at = pl.ds(pl.multiple_of(base + i * LANES + 8 * q, 8), 8)
-                t = [res[8 * q : 8 * q + 8, c * LANES : (c + 1) * LANES] + pot[c] for c in range(4)]
+                t = [part[8 * q : 8 * q + 8, :] + p for part, p in zip(found, pot)]
                 old = row_peak[at, :]
                 new = jnp.maximum(tree(jnp.maximum, t), old)
                 total = tree(jnp.add, [jnp.exp2(value - new) for value in t])
@@ -198,33 +201,27 @@
         relay(col ^ k, k).start()
     over_col(xbuf, sent.at[0], x_recv.at[0], 1).wait_recv()
     build_left(0)
-    build_right(0)
-    tile(my_x, my_z)
     over_col(xbuf, sent.at[0], x_recv.at[2], 4).wait_recv()
     relay(col ^ 4, 4).start()
+    build_right(0)
+    for level in range(4):
+        if level > 0:
+            k = 2 * gray(level)
+            relay(col ^ 1 ^ k, k).wait_recv()
+            build_left(level)
+        tile(my_x ^ gray(level), [my_z])
     build_right(1)
-    relay(col ^ 3, 2).wait_recv()
-    build_left(1)
-
-    def several(count, xs, zs):
-        def body(i, carry):
-            tile(xs(i), zs(i))
-            return carry
-
-        lax.fori_loop(0, count, body, 0)
-
-    several(3, lambda i: my_x ^ gray((i + 1) // 2), lambda i: my_z ^ gray(1 - i % 2))
+
+    def second(xg, carry):
+        tile(xg, [my_z ^ 1])
+        return carry
+
+    lax.fori_loop(0, 4, second, 0)
     build_right(2)
-    relay(col ^ 7, 6).wait_recv()
-    build_left(2)
-    several(5, lambda i: my_x ^ gray(jnp.minimum(i, 2)), lambda i: my_z ^ gray(jnp.where(i < 2, 2, i - 2)))
-    relay(col ^ 5, 4).wait_recv()
-    build_left(3)
-    several(3, lambda i: my_x ^ gray(3), lambda i: my_z ^ gray(i))
     build_right(3)
 
     def last(xg, carry):
-        tile(xg, my_z ^ gray(3))
+        tile(xg, [my_z ^ gray(2), my_z ^ gray(3)])
         for block in range(4):
             at = pl.ds(pl.multiple_of(xg * 512 + block * LANES, LANES), LANES)
             finish_rows(0, xg, block, row_peak[at, :], row_total[at, :])
@@ -287,21 +284,23 @@
                     top = jnp.max(peak, axis=0, keepdims=True)
                     whole = jnp.sum(total * jnp.exp2(peak - top), axis=0, keepdims=True)
                     lines.append(top + jnp.log2(whole))
-                vpart[step, quad // 2, row, pl.ds(quad % 2 * 4, 4), :] = jnp.concatenate(lines, axis=0)
-
-            @pl.when(jnp.logical_and(xg == 3, quad % 2 == 1))
+                vpart[step, quad, row] = jnp.concatenate(lines, axis=0)
+
+            @pl.when(xg == 3)
             def _():
-                half = quad // 2
                 for k in FAR_FIRST:
-                    over_row(vpart.at[step, half], sent.at[5 + step], v_recv.at[step, half], k).start()
+                    over_row(vpart.at[step, quad], sent.at[5 + step], v_recv.at[step, quad], k).start()
 
             return carry
 
         lax.fori_loop(0, GROUPS, body, 0)
 
     def combine_v(step, half):
-        all_of(vpart.at[step, half, 0 : ROWS - 1], v_recv.at[step, half]).wait()
-        parts = [vpart[step, half, k] for k in range(ROWS)]
+        for quad in range(2 * half, 2 * half + 2):
+            all_of(vpart.at[step, quad, 0 : ROWS - 1], v_recv.at[step, quad]).wait()
+        parts = [
+            jnp.concatenate([vpart[step, 2 * half, k], vpart[step, 2 * half + 1, k]], axis=0) for k in range(ROWS)
+        ]
         top = tree(jnp.maximum, parts)
         total = tree(jnp.add, [jnp.exp2(p - top) for p in parts])
         mass = jnp.concatenate([ybuf[8 * half + k, LATENT : LATENT + 1, :] for k in range(8)], axis=0)
@@ -370,7 +369,7 @@
             pltpu.VMEM((4, TERMS, 512), jnp.bfloat16),
             pltpu.VMEM((GROUPS, 2048, LANES), jnp.float32),
             pltpu.VMEM((2, 4, COLS, 4, LANES), jnp.float32),
-            pltpu.VMEM((2, 2, ROWS, 8, LANES), jnp.float32),
+            pltpu.VMEM((2, 4, ROWS, 4, LANES), jnp.float32),
             pltpu.VMEM((512, LANES), jnp.float32),
             pltpu.VMEM((2, GROUPS, 8, LANES), jnp.float32),
             pltpu.VMEM((2048, LANES), jnp.float32),
@@ -383,7 +382,7 @@
             pltpu.SemaphoreType.DMA((4,)),
             pltpu.SemaphoreType.DMA((4,)),
             pltpu.SemaphoreType.DMA((2, 4)),
-            pltpu.SemaphoreType.DMA((2, 2)),
+            pltpu.SemaphoreType.DMA((2, 4)),
         ],
         compiler_params=pltpu.CompilerParams(
             collective_id=0, has_side_effects=True, vmem_limit_bytes=48 * 1024 * 1024

time: 52.7 us -> 48.1 us (0.913)
  Pallas kernels: 51.2 us -> 46.7 us
    pallas_call x1, Pallas kernels: 51.2 us -> 46.7 us  [local(): pl.pallas_call(kernel, out_shape=(jax.ShapeDtypeStruct((GROUPS, LANES), j...]
where the time goes in v2:
time: 48.1 us; the launch traced here: 48 us
  Pallas kernels  46.7 us (97%)
  between operations  0.64 us (1%)
  other arithmetic  0.61 us (1%)
    pallas_call x1, Pallas kernels, local(): pl.pallas_call(kernel, out_shape=(jax.ShapeDtypeStruct((GROUPS, LANES), j...  46.7 us

profile of v2, /device:TPU:1, one launch (start us, length us, event | category | flops | bytes accessed | tf_op | source)
XLA Modules:
  0.0 48.0 jit_solution(8762653727958088368)
XLA Ops:
  0.6 46.7 %sinkhorn.1 = (f32[16,128]{1,0:T(8,128)S(1)}, f32[16,128]{1,0:T(8,128)S(1)}) custom-call(f32[64,256]{1,0:T(8,128)} %bitcast.8, f32[64,128]{1,0:T(8,128)} %bitcast.9, f32[2,128]{1,0:T(2,128)} %bitcast.10, f32[1,128]{1,0:T(1,128)} %bitcast.11, s32[2,2]{1,0:T(2,128)} %support_hbm.1), custom_call_target="tpu_custom_call" | custom-call | tf_op jit(solution)/shard_map/sinkhorn/pallas_call | solution.py:352
  47.4 0.6 %multiply_bitcast_fusion = (f32[2048]{0:T(1024)}, f32[2048]{0:T(1024)}) fusion(f32[16,128]{1,0:T(8,128)S(1)} %get-tuple-element.5, f32[16,128]{1,0:T(8,128)S(1)} %get-tuple-element.4), kind=kLoop, calls=%fused_computation | loop fusion | flops 4096 | bytes 32768 | tf_op jit(solution)/shard_map/mul | solution.py:403

commit v3 on v2

--- a/solution.py
+++ b/solution.py
@@ -61,14 +61,15 @@
             ((x_hbm, x_ref), (y_hbm, y_ref), (a_hbm, a_ref), (b_hbm, b_ref), (support_hbm, support_ref))
         )
     ]
-    for load in loads:
-        load.start()
 
     barrier = pltpu.get_barrier_semaphore()
     for k in FAR_FIRST:
         pl.semaphore_signal(barrier, inc=1, device_id=(row ^ k, col), device_id_type=MESH)
     for k in range(1, COLS):
         pl.semaphore_signal(barrier, inc=1, device_id=(row, col ^ k), device_id_type=MESH)
+
+    for load in loads:
+        load.start()
 
     def bias(a, b):
         return jnp.where(support_ref[a, b] == 1, jnp.float32(0.0), jnp.float32(NEGATIVE))
@@ -164,11 +165,17 @@
                     lower, high.astype(jnp.float32), low.astype(jnp.float32)
                 ).astype(jnp.bfloat16)
 
-    def tile(xg, zgs):
+    def finish_rows(step, xg, block, peak, total):
+        peak, total = peak.T, total.T
+        top = jnp.max(peak, axis=0, keepdims=True)
+        whole = jnp.sum(total * jnp.exp2(peak - top), axis=0, keepdims=True)
+        upart[step, xg, col, pl.ds(block, 1), :] = top + jnp.log2(whole)
+
+    def tile(xg, zgs, ending=False):
         pot = [vbias[xg // 2, zg * 4 + c] for zg in zgs for c in range(4)]
         base = xg * 512
         for i in range(4):
-            found = []
+            found, peaks, totals = [], [], []
             for zg in zgs:
                 res = jnp.dot(
                     left[xg, i * LANES : (i + 1) * LANES, :], right[zg], preferred_element_type=jnp.float32
@@ -183,17 +190,18 @@
                 old = row_peak[at, :]
                 new = jnp.maximum(tree(jnp.maximum, t), old)
                 total = tree(jnp.add, [jnp.exp2(value - new) for value in t])
-                row_total[at, :] = row_total[at, :] * jnp.exp2(old - new) + total
-                row_peak[at, :] = new
-
-    def finish_rows(step, xg, block, peak, total):
-        peak, total = peak.T, total.T
-        top = jnp.max(peak, axis=0, keepdims=True)
-        whole = jnp.sum(total * jnp.exp2(peak - top), axis=0, keepdims=True)
-        upart[step, xg, col, pl.ds(block, 1), :] = top + jnp.log2(whole)
+                total = row_total[at, :] * jnp.exp2(old - new) + total
+                if ending:
+                    peaks.append(new)
+                    totals.append(total)
+                else:
+                    row_total[at, :] = total
+                    row_peak[at, :] = new
+            if ending:
+                finish_rows(0, xg, i, jnp.concatenate(peaks, axis=0), jnp.concatenate(totals, axis=0))
 
     def send_u(step, xg):
-        for k in range(1, COLS):
+        for k in (4, 5, 2, 3, 6, 7, 1):
             over_col(upart.at[step, xg], sent.at[3 + step], u_recv.at[step, xg], k).start()
 
     for k in (2, 6):
@@ -221,10 +229,7 @@
     build_right(3)
 
     def last(xg, carry):
-        tile(xg, [my_z ^ gray(2), my_z ^ gray(3)])
-        for block in range(4):
-            at = pl.ds(pl.multiple_of(xg * 512 + block * LANES, LANES), LANES)
-            finish_rows(0, xg, block, row_peak[at, :], row_total[at, :])
+        tile(xg, [my_z ^ gray(2), my_z ^ gray(3)], ending=True)
         send_u(0, xg)
         return carry
 
@@ -249,13 +254,7 @@
         col_peak[...] = jnp.full((GROUPS, 8, LANES), 3.0 * NEGATIVE, jnp.float32)
         col_total[...] = jnp.zeros((GROUPS, 8, LANES), jnp.float32)
 
-        def body(t, carry):
-            xg, quad = t // 4, t % 4
-
-            @pl.when(quad == 0)
-            def _():
-                combine_u(step, xg)
-
+        def quad_pass(xg, quad):
             live = bias(xg // 2, quad // 2)
             base = xg * 512
             peaks = [[col_peak[4 * quad + c]] for c in range(4)]
@@ -270,30 +269,33 @@
                     peak = tree(jnp.maximum, values)
                     totals[c].append(tree(jnp.add, [jnp.exp2(value - peak) for value in values]))
                     peaks[c].append(peak + live)
-            for c in range(4):
-                top = tree(jnp.maximum, peaks[c])
-                total = tree(jnp.add, [q * jnp.exp2(p - top) for p, q in zip(peaks[c], totals[c])])
-                col_peak[4 * quad + c] = top
-                col_total[4 * quad + c] = total
-
-            @pl.when(xg == 3)
-            def _():
-                lines = []
+            tops = [tree(jnp.maximum, peaks[c]) for c in range(4)]
+            sums = [
+                tree(jnp.add, [q * jnp.exp2(p - tops[c]) for p, q in zip(peaks[c], totals[c])]) for c in range(4)
+            ]
+            return tops, sums
+
+        def body(xg, carry):
+            combine_u(step, xg)
+            for quad in range(4):
+                tops, sums = quad_pass(xg, quad)
                 for c in range(4):
-                    peak, total = col_peak[4 * quad + c], col_total[4 * quad + c]
-                    top = jnp.max(peak, axis=0, keepdims=True)
-                    whole = jnp.sum(total * jnp.exp2(peak - top), axis=0, keepdims=True)
-                    lines.append(top + jnp.log2(whole))
-                vpart[step, quad, row] = jnp.concatenate(lines, axis=0)
-
-            @pl.when(xg == 3)
-            def _():
-                for k in FAR_FIRST:
-                    over_row(vpart.at[step, quad], sent.at[5 + step], v_recv.at[step, quad], k).start()
-
+                    col_peak[4 * quad + c] = tops[c]
+                    col_total[4 * quad + c] = sums[c]
             return carry
 
-        lax.fori_loop(0, GROUPS, body, 0)
+        lax.fori_loop(0, 3, body, 0)
+        combine_u(step, 3)
+        for quad in range(4):
+            tops, sums = quad_pass(3, quad)
+            lines = []
+            for peak, total in zip(tops, sums):
+                top = jnp.max(peak, axis=0, keepdims=True)
+                whole = jnp.sum(total * jnp.exp2(peak - top), axis=0, keepdims=True)
+                lines.append(top + jnp.log2(whole))
+            vpart[step, quad, row] = jnp.concatenate(lines, axis=0)
+            for k in FAR_FIRST:
+                over_row(vpart.at[step, quad], sent.at[5 + step], v_recv.at[step, quad], k).start()
 
     def combine_v(step, half):
         for quad in range(2 * half, 2 * half + 2):
@@ -314,25 +316,20 @@
             for c in range(8):
                 vbias[a, 8 * half + c] = jnp.broadcast_to(shifted[c : c + 1, :], (8, LANES))
 
-    def row_block(t, carry):
-        xg, block = t // 4, t % 4
-        pot = [vbias[xg // 2, c] for c in range(GROUPS)]
-        peaks, totals = [], []
-        for k in range(GROUPS):
-            at = pl.ds(pl.multiple_of(t * LANES + 8 * k, 8), 8)
-            values = [score[c, at, :] + pot[c] for c in range(GROUPS)]
-            peak = tree(jnp.maximum, values)
-            totals.append(tree(jnp.add, [jnp.exp2(value - peak) for value in values]))
-            peaks.append(peak)
-        finish_rows(1, xg, block, jnp.concatenate(peaks, axis=0), jnp.concatenate(totals, axis=0))
-
-        @pl.when(block == 3)
-        def _():
-            send_u(1, xg)
-
+    def row_blocks(xg, carry):
+        for block in range(4):
+            pot = [vbias[xg // 2, c] for c in range(GROUPS)]
+            peaks, totals = [], []
+            for k in range(GROUPS):
+                at = pl.ds(pl.multiple_of(xg * 512 + block * LANES + 8 * k, 8), 8)
+                values = [score[c, at, :] + pot[c] for c in range(GROUPS)]
+                peaks.append(tree(jnp.maximum, values))
+                totals.append(tree(jnp.add, [jnp.exp2(value - peaks[-1]) for value in values]))
+            finish_rows(1, xg, block, jnp.concatenate(peaks, axis=0), jnp.concatenate(totals, axis=0))
+        send_u(1, xg)
         return carry
 
-    lax.fori_loop(0, GROUPS, row_block, 0)
+    lax.fori_loop(0, 4, row_blocks, 0)
     column_pass(1)
     all_of(xbuf.at[0:4], sent.at[0]).wait()
     all_of(xbuf.at[0:3], sent.at[1]).wait()

time: 48.1 us -> 45.9 us (0.954)
  Pallas kernels: 46.7 us -> 44.5 us
    pallas_call x1, Pallas kernels: 46.7 us -> 44.5 us  [local(): pl.pallas_call(kernel, out_shape=(jax.ShapeDtypeStruct((GROUPS, LANES), j...]
where the time goes in v3:
time: 45.9 us; the launch traced here: 45.7 us
  Pallas kernels  44.5 us (97%)
  between operations  0.64 us (1%)
  other arithmetic  0.61 us (1%)
    pallas_call x1, Pallas kernels, local(): pl.pallas_call(kernel, out_shape=(jax.ShapeDtypeStruct((GROUPS, LANES), j...  44.5 us

profile of v3, /device:TPU:1, one launch (start us, length us, event | category | flops | bytes accessed | tf_op | source)
XLA Modules:
  0.0 45.7 jit_solution(11532782880288377227)
XLA Ops:
  0.6 44.5 %sinkhorn.1 = (f32[16,128]{1,0:T(8,128)S(1)}, f32[16,128]{1,0:T(8,128)S(1)}) custom-call(f32[64,256]{1,0:T(8,128)} %bitcast.8, f32[64,128]{1,0:T(8,128)} %bitcast.9, f32[2,128]{1,0:T(2,128)} %bitcast.10, f32[1,128]{1,0:T(1,128)} %bitcast.11, s32[2,2]{1,0:T(2,128)} %support_hbm.1), custom_call_target="tpu_custom_call" | custom-call | tf_op jit(solution)/shard_map/sinkhorn/pallas_call | solution.py:349
  45.1 0.6 %multiply_bitcast_fusion = (f32[2048]{0:T(1024)}, f32[2048]{0:T(1024)}) fusion(f32[16,128]{1,0:T(8,128)S(1)} %get-tuple-element.5, f32[16,128]{1,0:T(8,128)S(1)} %get-tuple-element.4), kind=kLoop, calls=%fused_computation | loop fusion | flops 4096 | bytes 32768 | tf_op jit(solution)/shard_map/mul | solution.py:400

commit v4 on v3

--- a/solution.py
+++ b/solution.py
@@ -166,9 +166,9 @@
                 ).astype(jnp.bfloat16)
 
     def finish_rows(step, xg, block, peak, total):
-        peak, total = peak.T, total.T
-        top = jnp.max(peak, axis=0, keepdims=True)
-        whole = jnp.sum(total * jnp.exp2(peak - top), axis=0, keepdims=True)
+        value = (peak + jnp.log2(total)).T
+        top = jnp.max(value, axis=0, keepdims=True)
+        whole = jnp.sum(jnp.exp2(value - top), axis=0, keepdims=True)
         upart[step, xg, col, pl.ds(block, 1), :] = top + jnp.log2(whole)
 
     def tile(xg, zgs, ending=False):

time: 45.9 us -> 45.8 us (level)
  no operation moved by 1% of the time
where the time goes in v4:
time: 45.8 us; the launch traced here: 45.7 us
  Pallas kernels  44.4 us (97%)
  between operations  0.64 us (1%)
  other arithmetic  0.61 us (1%)
    pallas_call x1, Pallas kernels, local(): pl.pallas_call(kernel, out_shape=(jax.ShapeDtypeStruct((GROUPS, LANES), j...  44.4 us

profile of v4, /device:TPU:1, one launch (start us, length us, event | category | flops | bytes accessed | tf_op | source)
XLA Modules:
  0.0 45.7 jit_solution(13033518343423559859)
XLA Ops:
  0.6 44.4 %sinkhorn.1 = (f32[16,128]{1,0:T(8,128)S(1)}, f32[16,128]{1,0:T(8,128)S(1)}) custom-call(f32[64,256]{1,0:T(8,128)} %bitcast.8, f32[64,128]{1,0:T(8,128)} %bitcast.9, f32[2,128]{1,0:T(2,128)} %bitcast.10, f32[1,128]{1,0:T(1,128)} %bitcast.11, s32[2,2]{1,0:T(2,128)} %support_hbm.1), custom_call_target="tpu_custom_call" | custom-call | tf_op jit(solution)/shard_map/sinkhorn/pallas_call | solution.py:349
  45.1 0.6 %multiply_bitcast_fusion = (f32[2048]{0:T(1024)}, f32[2048]{0:T(1024)}) fusion(f32[16,128]{1,0:T(8,128)S(1)} %get-tuple-element.5, f32[16,128]{1,0:T(8,128)S(1)} %get-tuple-element.4), kind=kLoop, calls=%fused_computation | loop fusion | flops 4096 | bytes 32768 | tf_op jit(solution)/shard_map/mul | solution.py:400
